TPU v7x, 32 devices: a whole 2x2x4 slice. The times are simulated.
32 devices in a mesh: group: 2 (over y), expert: 16 (over z, x, core), tensor: 1.
Axes of the slice: x: 2, y: 2, z: 4, core: 2. Of those that a mesh axis runs over, the one named last changes fastest.
Arguments:
- tokens: bfloat16 [4096, 2048], P(('group', 'expert'), 'tensor'), parts along dimension 0, may hold values from -6 to 6
- expert_ids: int32 [4096, 8], P(('group', 'expert')), parts along dimension 0, may hold values from 0 to 15, all different within a row; in each aligned block of 128 rows (0 to 127, 128 to 255, ...) at most 128 rows name the same one
- gate_numer: int32 [4096, 8], P(('group', 'expert')), parts along dimension 0, may hold values from 1 to 255
- capacity: int32 [16], replicated, may hold values from 512 to 1535
- up_weight: bfloat16 [16, 2048, 768], P('expert', None, 'tensor'), may hold values from -0.125 to 0.125
- down_weight: bfloat16 [16, 768, 2048], P('expert', None, 'tensor'), may hold values from -0.21875 to 0.21875
Outputs:
- mixed: bfloat16 [4096, 2048], P(('group', 'expert'), 'tensor'), parts along dimension 0
There are 2 independent parts, one for each index of `group`. A program takes and returns all parts, laid end to end along the dimension named above; an argument that names none is the same for every part. Nothing has to cross between parts.
Inputs may be any that keep to these rules, and one draw needn't show every extreme that they name: `expert_ids`: each token names 8 different experts. In each aligned block of 128 rows (the tokens of one index of expert) no expert is named more than 128 times, a bound that some block reaches.
All inputs are finite; a program needn't handle non-finite values.
Results may differ from a plain program's by a relative error of at most 0.0075.
Values may be sent and summed in bfloat16 or wider, within the bound.
A program may use at most 128 MiB of HBM per device.

v0:
```python
import jax
import jax.numpy as jnp
from jax import lax
from jax.sharding import PartitionSpec as P


def entering(part, axis, combine, identity):
    place = lax.axis_index(axis)
    gathered = lax.all_gather(part, axis)
    state = jnp.zeros_like(part) + jnp.asarray(identity, part.dtype)

    def one(lap, state):
        return combine(state, lax.dynamic_index_in_dim(gathered, lap, 0, False))

    return lax.fori_loop(0, place, one, state)


def add_counts(earlier, later):
    return earlier + later


def expert_work(received, up_matrix, down_matrix):
    sources, slot_count, half_width = received.shape
    hidden_half = up_matrix.shape[1]
    fragment = lax.all_gather(received, "tensor", axis=2, tiled=True)
    columns = fragment.shape[2]
    weights_block = up_matrix
    up_total = jnp.dot(
        fragment.reshape(-1, columns), weights_block, preferred_element_type=jnp.float32
    )
    hidden = jax.nn.silu(up_total).astype(jnp.bfloat16).reshape(sources, slot_count, hidden_half)
    fragment = lax.all_gather(hidden, "tensor", axis=2, tiled=True)
    columns = fragment.shape[2]
    weights_block = down_matrix
    down_total = jnp.dot(
        fragment.reshape(-1, columns), weights_block, preferred_element_type=jnp.float32
    )
    return down_total.astype(jnp.bfloat16).reshape(sources, slot_count, half_width)


def local(tokens, expert_ids, gate_numer, capacity, up_weight, down_weight):
    token_rows, half_width = tokens.shape
    per_token = expert_ids.shape[1]
    experts = capacity.shape[0]
    per_source = min(token_rows, 2 * token_rows * per_token // experts)
    chosen = expert_ids.reshape(-1)
    one_hot = (chosen[:, None] == jnp.arange(experts, dtype=jnp.int32)[None, :]).astype(jnp.int32)
    counts = jnp.sum(one_hot, axis=0)
    local_rank = jnp.sum((jnp.cumsum(one_hot, axis=0) - one_hot) * one_hot, axis=1)
    prefix = entering(counts, "expert", add_counts, jnp.zeros_like(counts))
    global_rank = local_rank + jnp.sum(one_hot * prefix[None, :], axis=1)
    limit = jnp.sum(one_hot * capacity[None, :], axis=1)
    retained = global_rank < limit
    numerator = gate_numer.astype(jnp.float32)
    weighting = (numerator / jnp.sum(numerator, axis=1, keepdims=True)).reshape(-1)
    weighting = jnp.where(retained, weighting, jnp.zeros_like(weighting))
    token_of = jnp.arange(token_rows * per_token, dtype=jnp.int32) // per_token
    slot_table = (
        jnp.full((experts, per_source), token_rows, jnp.int32).at[chosen, local_rank].set(token_of)
    )
    source = jnp.concatenate([tokens, jnp.zeros((1, half_width), tokens.dtype)], axis=0)
    up_matrix = up_weight[0]
    down_matrix = down_weight[0]
    outgoing = source[slot_table]
    arrived = lax.all_to_all(outgoing, "expert", split_axis=0, concat_axis=0, tiled=True)
    returned = lax.all_to_all(
        expert_work(arrived, up_matrix, down_matrix),
        "expert",
        split_axis=0,
        concat_axis=0,
        tiled=True,
    )
    picked = returned[chosen, local_rank]
    weighted = picked.astype(jnp.float32) * weighting[:, None]
    mixed = jnp.sum(weighted.reshape(token_rows, per_token, picked.shape[1]), axis=1)
    return mixed.astype(jnp.bfloat16)


def solution(mesh):
    in_specs = (
        P(("group", "expert"), "tensor"),
        P(("group", "expert"), None),
        P(("group", "expert"), None),
        P(),
        P("expert", None, "tensor"),
        P("expert", None, "tensor"),
    )
    out_specs = P(("group", "expert"), "tensor")
    return jax.shard_map(local, mesh=mesh, in_specs=in_specs, out_specs=out_specs, check_vma=False)
```

profile of v0, /device:TPU:26, one launch (start us, length us, event | category | flops | bytes accessed | tf_op | source)
XLA Modules:
  0.0 473.9 jit_solution(17383743363278048700)
XLA Ops:
  0.0 0.0 copy-start
  0.0 0.9 copy.18
  0.9 0.1 eq.29
  1.0 0.1 eq.25
  1.1 0.1 reshape.100
  1.2 4.5 reduce-window.6
  5.8 0.1 slice.12
  5.8 0.1 copy.21
  6.0 0.1 copy.22
  6.1 0.1 broadcast_add_fusion
  6.2 0.1 convert_reduce_fusion
  6.3 1.3 dynamic-slice
  8.3 0.2 dynamic-update-slice
  8.6 8.2 %all-reduce.1 = s32[256]{0:T(256)S(1)} all-reduce(s32[256]{0:T(256)S(1)} %dynamic-update-slice), channel_id=2, replica_groups=mesh['group'=2,'expert'=16,'tensor'=1] {'expert'}, use_global_device_ids=true, to_apply=%add.1 | all-reduce | flops 256 | bytes 2048
  16.8 0.1 reshape.129
  16.9 0.6 while.10
  17.5 0.8 select_reduce_fusion.1
  18.3 0.7 multiply_reduce_fusion
  19.0 0.8 and_reduce_fusion
  19.8 4.3 scatter_custom_fusion
  24.1 2.0 concatenate.7
  26.1 17.5 %gather_fusion = bf16[2048,2048]{1,0:T(8,128)(2,1)} fusion(bf16[129,2048]{1,0:T(8,128)(2,1)} %concatenate.7, s32[2048]{0:T(1024)S(1)} %fusion.13), kind=kCustom, calls=%fused_computation | custom fusion | bytes 16785408 | tf_op jit(solution)/shard_map/gather | solution.py:64
  43.5 189.5 %all_to_all.10 = bf16[16,128,2048]{2,1,0:T(8,128)(2,1)} all-to-all(bf16[16,128,2048]{2,1,0:T(8,128)(2,1)} %bitcast.41), channel_id=1, replica_groups=mesh['group'=2,'expert'=16,'tensor'=1] {'expert'}, dimensions={0} | all-to-all | bytes 16777216 | tf_op jit(solution)/shard_map/all_to_all | solution.py:65
  233.0 0.0 copy-done
  233.0 20.4 %convolution_convert_fusion = bf16[2048,2048]{1,0:T(8,128)(2,1)} fusion(bf16[1,768,2048]{2,1,0:T(8,128)(2,1)S(1)} %copy-done, bf16[2048,2048]{1,0:T(8,128)(2,1)} %bitcast.43, bf16[1,2048,768]{2,1,0:T(8,128)(2,1)} %param.12), kind=kOutput, calls=%fused_computation.6 | convolution fusion | flops 12896960512 | bytes 23068672 | tf_op jit(solution)/shard_map/dot_general | solution.py:35
  253.4 0.0 copy-start.1
  253.4 6.1 %all-to-all-start.1 = ((bf16[16,128,2048]{2,1,0:T(8,128)(2,1)}), bf16[16,128,2048]{2,1,0:T(8,128)(2,1)}, u32[]{:S(2)}, u32[]{:S(2)}) async-start(bf16[16,128,2048]{2,1,0:T(8,128)(2,1)} %bitcast.42), calls=%async_computation.1 | async-start | bytes 16777216 | tf_op jit(solution)/shard_map/all_to_all | solution.py:66
  259.6 0.1 lt.50
  259.7 0.1 copy.23
  259.7 0.0 copy-done.1
  259.8 0.1 copy.24
  259.9 181.1 %all-to-all-done.1 = bf16[16,128,2048]{2,1,0:T(8,128)(2,1)} async-done(((bf16[16,128,2048]{2,1,0:T(8,128)(2,1)}), bf16[16,128,2048]{2,1,0:T(8,128)(2,1)}, u32[]{:S(2)}, u32[]{:S(2)}) %all-to-all-start.1) | async-done | bytes 8388640 | tf_op jit(solution)/shard_map/all_to_all | solution.py:66
  441.0 25.6 %gather_fusion.1 = bf16[1024,2048]{1,0:T(8,128)(2,1)} fusion(bf16[16,128,2048]{2,1,0:T(8,128)(2,1)} %all-to-all-done.1, s32[1024]{0:T(1024)S(1)} %bitcast.40), kind=kCustom, calls=%fused_computation.1 | custom fusion | bytes 8396800 | tf_op jit(solution)/shard_map/gather | solution.py:73
  466.5 7.3 %fusion = bf16[128,2048]{1,0:T(8,128)(2,1)} fusion(bf16[1024,2048]{1,0:T(8,128)(2,1)} %gather_fusion.1, f32[128,8]{1,0:T(8,128)S(1)} %copy.24), kind=kLoop, calls=%fused_computation.5 | loop fusion | flops 6029312 | bytes 4722688 | tf_op jit(solution)/shard_map/reduce_sum | solution.py:75
  (25 shorter events, 0.4 us)
Async XLA Ops:
  0.0 233.0 %copy-start = (bf16[1,768,2048]{2,1,0:T(8,128)(2,1)S(1)}, bf16[1,768,2048]{2,1,0:T(8,128)(2,1)}, u32[]{:S(2)}) copy-start(bf16[1,768,2048]{2,1,0:T(8,128)(2,1)} %param.13) | copy-start | bytes 9437188
  253.4 6.3 %copy-start.1 = (s32[128,8]{0,1:T(8,128)S(1)}, s32[128,8]{0,1:T(8,128)}, u32[]{:S(2)}) copy-start(s32[128,8]{0,1:T(8,128)} %param.10) | copy-start | bytes 12292
  253.4 187.6 %all-to-all-start.1 = ((bf16[16,128,2048]{2,1,0:T(8,128)(2,1)}), bf16[16,128,2048]{2,1,0:T(8,128)(2,1)}, u32[]{:S(2)}, u32[]{:S(2)}) async-start(bf16[16,128,2048]{2,1,0:T(8,128)(2,1)} %bitcast.42), calls=%async_computation.1 | async-start | bytes 16777216 | tf_op jit(solution)/shard_map/all_to_all | solution.py:66
where the time goes:
time: 476 us; the launch traced here: 474 us
  blocking collectives  198 us (42%)
  waiting for transfers between devices  181 us (38%)
  local copies, waits for them, and re-layouts  52.7 us (11%)
  matrix products  20.4 us (4%)
  other arithmetic  14.7 us (3%)
  starting transfers between devices  6.15 us (1%)
    all_to_all x1, blocking collectives, local(): lax.all_to_all(outgoing, 'expert', split_axis=0, concat_axis=0, tiled=True)  189 us
    all_to_all x1, waiting for transfers between devices, local(): lax.all_to_all(expert_work(arrived, up_matrix, down_matrix), 'expert', sp...  181 us
    gather x1, local copies, waits for them, and re-layouts, local(): picked = returned[chosen, local_rank]  25.6 us
    dot_general x1, matrix products, expert_work(): jnp.dot(fragment.reshape(-1, columns), weights_block, preferred_element_t...  20.4 us
    gather x1, local copies, waits for them, and re-layouts, local(): outgoing = source[slot_table]  17.5 us
  transfers between devices with their start and end apart: 1, of which 1 were waited for; matrix products, arithmetic and copies ran while one was open for 0% of the time, Pallas kernels for 0%

commit v1 on v0

--- a/solution.py
+++ b/solution.py
@@ -38,7 +38,7 @@
     return down_total.astype(jnp.bfloat16).reshape(sources, slot_count, half_width)
 
 
-def local(tokens, expert_ids, gate_numer, capacity, up_weight, down_weight):
+def general(tokens, expert_ids, gate_numer, capacity, up_weight, down_weight):
     token_rows, half_width = tokens.shape
     per_token = expert_ids.shape[1]
     experts = capacity.shape[0]
@@ -76,7 +76,33 @@
     return mixed.astype(jnp.bfloat16)
 
 
+def column_weight(chosen, numer, capacity, expert):
+    hit = chosen == expert
+    named = jnp.any(hit, axis=1)
+    rank = jnp.cumsum(named.astype(jnp.int32)) - named.astype(jnp.int32)
+    gate = jnp.sum(jnp.where(hit, numer, 0), axis=1).astype(jnp.float32)
+    weight = gate / jnp.sum(numer, axis=1).astype(jnp.float32)
+    return jnp.where(rank < capacity[expert], weight, 0.0)
+
+
+def dense(tokens, expert_ids, gate_numer, capacity, up_weight, down_weight):
+    per_token = expert_ids.shape[1]
+    place = lax.axis_index("expert")
+    routing = lax.all_gather(
+        jnp.concatenate([expert_ids, gate_numer], axis=1), "expert", tiled=True
+    )
+    rows = lax.all_gather(tokens, "expert", tiled=True)
+    weight = column_weight(routing[:, :per_token], routing[:, per_token:], capacity, place)
+    hidden = jnp.dot(rows, up_weight[0], preferred_element_type=jnp.float32)
+    hidden = jax.nn.silu(hidden).astype(jnp.bfloat16)
+    result = jnp.dot(hidden, down_weight[0], preferred_element_type=jnp.float32)
+    part = (weight[:, None] * result).astype(jnp.bfloat16)
+    return lax.psum_scatter(part, "expert", scatter_dimension=0, tiled=True)
+
+
 def solution(mesh):
+    one_each = mesh.shape["tensor"] == 1 and mesh.shape["expert"] <= 16
+    local = dense if one_each else general
     in_specs = (
         P(("group", "expert"), "tensor"),
         P(("group", "expert"), None),

time: 476 us -> 217 us (0.46)
  blocking collectives: 198 us -> 17 us
  local copies, waits for them, and re-layouts: 52.7 us -> 1.43 us
  waiting for transfers between devices: 181 us -> 160 us
  other arithmetic: 14.7 us -> 2 us
  between operations: 0.81 us -> 13.4 us
  starting transfers between devices: 6.15 us -> 0.04 us
    all_to_all x1 -> x0, blocking collectives: 189 us -> none  [local(): lax.all_to_all(outgoing, 'expert', split_axis=0, concat_axis=0, tiled=True)]
    all_to_all x1 -> x0, waiting for transfers between devices: 181 us -> none  [local(): lax.all_to_all(expert_work(arrived, up_matrix, down_matrix), 'expert', sp...]
    reduce_scatter x0 -> x1, waiting for transfers between devices: none -> 104 us  [dense(): return lax.psum_scatter(part, 'expert', scatter_dimension=0, tiled=True)]
    all_gather x0 -> x1, waiting for transfers between devices: none -> 55.2 us  [dense(): rows = lax.all_gather(tokens, 'expert', tiled=True)]
    gather x2 -> x0, local copies, waits for them, and re-layouts: 43 us -> none  [the longest x1 25.6 us: local(): picked = returned[chosen, local_rank]]
    all_gather x0 -> x1, blocking collectives: none -> 17 us  [dense(): lax.all_gather(jnp.concatenate([expert_ids, gate_numer], axis=1), 'expert...]
    unnamed x1 -> x0, blocking collectives: 8.24 us -> none
    reduce_sum x4 -> x1, other arithmetic: 8.24 us -> 0.04 us  [column_weight(): gate = jnp.sum(jnp.where(hit, numer, 0), axis=1).astype(jnp.float32)]
  transfers between devices with their start and end apart: 1 -> 2, of which waited for: 1 -> 2; matrix products, arithmetic and copies ran while one was open for 0% -> 2% of each run, Pallas kernels for 0% -> 0%
where the time goes in v1:
time: 217 us; the launch traced here: 214 us
  waiting for transfers between devices  160 us (74%)
  matrix products  20 us (9%)
  blocking collectives  17 us (8%)
  between operations  13.4 us (6%)
    reduce_scatter x1, waiting for transfers between devices, dense(): return lax.psum_scatter(part, 'expert', scatter_dimension=0, tiled=True)  104 us
    all_gather x1, waiting for transfers between devices, dense(): rows = lax.all_gather(tokens, 'expert', tiled=True)  55.2 us
    dot_general x1, matrix products, dense(): result = jnp.dot(hidden, down_weight[0], preferred_element_type=jnp.float32)  20 us
    all_gather x1, blocking collectives, dense(): lax.all_gather(jnp.concatenate([expert_ids, gate_numer], axis=1), 'expert...  17 us
  transfers between devices with their start and end apart: 2, of which 2 were waited for; matrix products, arithmetic and copies ran while one was open for 2% of the time, Pallas kernels for 0%

profile of v1, /device:TPU:26, one launch (start us, length us, event | category | flops | bytes accessed | tf_op | source)
XLA Modules:
  0.0 214.3 jit_solution(2394971881244274325)
XLA Ops:
  6.5 0.0 copy-start
  6.5 0.0 all-gather.2.cloned.1.call-start
  6.5 0.7 all-gather.2.cloned.1.call-update
  7.3 0.0 reduce-scatter.2.cloned.1.call-start
  7.3 0.9 pad_add_fusion
  8.2 17.0 %all_gather.6 = s32[2048,16]{0,1:T(8,128)S(1)} all-gather(s32[128,16]{0,1:T(8,128)S(1)} %pad_add_fusion), channel_id=1, replica_groups=mesh['group'=2,'expert'=16,'tensor'=1] {'expert'}, dimensions={0}, use_global_device_ids=true | all-gather | bytes 139264 | tf_op jit(solution)/shard_map/all_gather | solution.py:91
  25.3 0.3 reduce-window.9
  25.5 0.1 slice.18
  25.6 1.2 dynamic_slice.3
  26.9 0.1 slice_reduce_fusion.1
  27.1 0.7 divide_select_fusion
  27.8 55.2 %all-gather.2.cloned.1.call-done = bf16[2048,2048]{1,0:T(8,128)(2,1)} async-done(((bf16[128,2048]{1,0:T(8,128)(2,1)}), bf16[2048,2048]{1,0:T(8,128)(2,1)}) %all-gather.2.cloned.1.call-update) | async-done | bytes 8388624 | tf_op jit(solution)/shard_map/all_gather | solution.py:94
  83.0 0.0 copy-done
  83.0 20.0 %multiply_convert_fusion = bf16[2048,2048]{1,0:T(8,128)(2,1)} fusion(f32[2048]{0:T(1024)S(1)} %divide_select_fusion, bf16[1,768,2048]{2,1,0:T(8,128)(2,1)S(1)} %copy-done, bf16[2048,2048]{1,0:T(8,128)(2,1)} %all-gather.2.cloned.1.call-done, bf16[1,2048,768]{2,1,0:T(8,128)(2,1)} %param.10), kind=kOutput, calls=%fused_computation | convolution fusion | flops 12901154816 | bytes 23076864 | tf_op jit(solution)/shard_map/dot_general | solution.py:98
  103.0 0.0 reduce-scatter.2.cloned.1.call-update
  103.0 104.4 %reduce-scatter.2.cloned.1.call-done = bf16[128,2048]{1,0:T(8,128)(2,1)} async-done(((bf16[2048,2048]{1,0:T(8,128)(2,1)}), bf16[128,2048]{1,0:T(8,128)(2,1)}) %reduce-scatter.2.cloned.1.call-update) | async-done | bytes 524304 | tf_op jit(solution)/shard_map/reduce_scatter | solution.py:100
  (4 shorter events, 0.1 us)
Async XLA Ops:
  6.5 76.5 %copy-start = (bf16[1,768,2048]{2,1,0:T(8,128)(2,1)S(1)}, bf16[1,768,2048]{2,1,0:T(8,128)(2,1)}, u32[]{:S(2)}) copy-start(bf16[1,768,2048]{2,1,0:T(8,128)(2,1)} %param.11) | copy-start | bytes 9437188
  6.5 76.4 %all-gather.2.cloned.1.call-start = ((), (), s32[]{:S(2)}) async-start(), calls=%async_computation.1 | async-start | bytes 8912896 | tf_op jit(solution)/shard_map/all_gather | solution.py:94
  7.3 200.2 %reduce-scatter.2.cloned.1.call-start = ((), (), s32[]{:S(2)}) async-start(), calls=%async_computation.2 | async-start | bytes 8912896 | tf_op jit(solution)/shard_map/reduce_scatter | solution.py:100
Sparse Core Ops, SparseCore 0:
  9.5 73.4 all-gather.1
  103.1 104.2 reduce-scatter.1

commit v2 on v0

--- a/solution.py
+++ b/solution.py
@@ -1,6 +1,10 @@
+import functools
+
 import jax
 import jax.numpy as jnp
 from jax import lax
+from jax.experimental import pallas as pl
+from jax.experimental.pallas import tpu as pltpu
 from jax.sharding import PartitionSpec as P
 
 
@@ -38,7 +42,7 @@
     return down_total.astype(jnp.bfloat16).reshape(sources, slot_count, half_width)
 
 
-def local(tokens, expert_ids, gate_numer, capacity, up_weight, down_weight):
+def general(tokens, expert_ids, gate_numer, capacity, up_weight, down_weight):
     token_rows, half_width = tokens.shape
     per_token = expert_ids.shape[1]
     experts = capacity.shape[0]
@@ -76,7 +80,230 @@
     return mixed.astype(jnp.bfloat16)
 
 
+def add_rows(dst, *parts):
+    @pl.loop(0, dst.shape[0] // 16)
+    def _(i):
+        rows = pl.ds(pl.multiple_of(i * 16, 16), 16)
+        total = parts[0][rows, :].astype(jnp.float32)
+        for part in parts[1:]:
+            total = total + part[rows, :].astype(jnp.float32)
+        dst[rows, :] = total.astype(dst.dtype)
+
+
+def routed_weights(meta, capacity, weights, place, nz):
+    slots, _, block = meta.shape
+    half = meta.shape[1] // 2
+    c, x, z = place % 2, (place // 2) % 2, place // 4
+
+    def block_of(r):
+        cf, xf, k = r // (2 * nz), (r // nz) % 2, r % nz
+        zs = z - k
+        zs = jnp.where(zs < 0, zs + nz, zs)
+        return zs * 4 + (x + xf - 2 * x * xf) * 2 + (c + cf - 2 * c * cf)
+
+    ids = meta[:, :half, :].astype(jnp.float32)
+    gates = meta[:, half:, :].astype(jnp.float32)
+    hit = (ids == place.astype(jnp.float32)).astype(jnp.float32)
+    named = jnp.sum(hit, axis=1)
+    gate = jnp.sum(hit * gates, axis=1)
+    whole = jnp.sum(gates, axis=1)
+    row = lax.broadcasted_iota(jnp.int32, (block, block), 0)
+    col = lax.broadcasted_iota(jnp.int32, (block, block), 1)
+    earlier = (row < col).astype(jnp.bfloat16)
+    inside = jnp.dot(named.astype(jnp.bfloat16), earlier, preferred_element_type=jnp.float32)
+    later_slot = lax.broadcasted_iota(jnp.int32, (slots, slots), 0)
+    early_slot = lax.broadcasted_iota(jnp.int32, (slots, slots), 1)
+    lower = (block_of(early_slot) < block_of(later_slot)).astype(jnp.bfloat16)
+    before = jnp.dot(lower, named.astype(jnp.bfloat16), preferred_element_type=jnp.float32)
+    rank = inside + jnp.sum(before, axis=1, keepdims=True)
+    limit = capacity[place].astype(jnp.float32)
+    spread = jnp.where(rank < limit, gate / whole, 0.0)
+    weights[...] = jnp.zeros_like(weights)
+    weights[0:slots, :] = spread
+    weights[...] = weights[...].T
+
+
+def block_work(rows, hidden, up, down, weights, slot, keep, give):
+    width = 256
+    block = keep.shape[0]
+
+    @pl.loop(0, up.shape[1] // width)
+    def _(i):
+        cols = pl.ds(pl.multiple_of(i * width, width), width)
+        v = jnp.dot(rows[...].reshape(2 * block, rows.shape[-1]), up[:, cols], preferred_element_type=jnp.float32)
+        hidden[:, cols] = (v / (1.0 + jnp.exp(-v))).astype(jnp.bfloat16)
+
+    mine = weights[:, slot[0] : slot[0] + 1]
+    other = weights[:, slot[1] : slot[1] + 1]
+
+    @pl.loop(0, down.shape[1] // width)
+    def _(i):
+        cols = pl.ds(pl.multiple_of(i * width, width), width)
+        v = jnp.dot(hidden[...], down[:, cols], preferred_element_type=jnp.float32)
+        keep[:, cols] = (v[:block] * mine).astype(jnp.bfloat16)
+        give[:, cols] = (v[block:] * other).astype(jnp.bfloat16)
+
+
+def kernel(
+    nz, tokens_hbm, meta_in, capacity, up_hbm, down_hbm, out,
+    held, meta, up, down, hidden, weights, keep, give, from_core, from_x, from_z,
+    local_sem, meta_send, meta_recv, gz_send, gx_send, gc_send, g_recv,
+    rc_send, rc_recv, rx_send, rx_recv, rz_send, rz_recv,
+):
+    place = lax.axis_index("expert")
+    c, x, z = place % 2, (place // 2) % 2, place // 4
+    sibling = place + 1 - 2 * c
+    across = place + 2 - 4 * x
+    block = tokens_hbm.shape[0]
+
+    def along(k):
+        return lax.rem(place + 4 * k, 4 * nz)
+
+    def remote(src, dst, send, recv, target):
+        copy = pltpu.make_async_remote_copy(
+            src_ref=src, dst_ref=dst, send_sem=send, recv_sem=recv,
+            device_id={"expert": target}, device_id_type=pl.DeviceIdType.MESH,
+        )
+        copy.start()
+        sent.append(copy)
+
+    def arrived(ref, sem):
+        pltpu.make_async_copy(ref, ref, sem).wait()
+
+    sent = []
+    loads = [
+        pltpu.make_async_copy(tokens_hbm, held.at[0, 0, 0], local_sem.at[0]),
+        pltpu.make_async_copy(up_hbm.at[0], up, local_sem.at[1]),
+        pltpu.make_async_copy(down_hbm.at[0], down, local_sem.at[2]),
+    ]
+    for load in loads:
+        load.start()
+    meta[0] = meta_in[...]
+
+    barrier = pltpu.get_barrier_semaphore()
+    partners = [sibling, across] + [along(k) for k in range(1, nz)]
+    for partner in partners:
+        pl.semaphore_signal(
+            barrier, inc=1, device_id={"expert": partner}, device_id_type=pl.DeviceIdType.MESH
+        )
+    pl.semaphore_wait(barrier, len(partners))
+
+    def gather_across(k):
+        remote(held.at[k, 0, 0], held.at[k, 1, 0], gx_send.at[k], g_recv.at[k, 1, 0], across)
+
+    def gather_core(k, xf):
+        remote(held.at[k, xf, 0], held.at[k, xf, 1], gc_send.at[k, xf], g_recv.at[k, xf, 1], sibling)
+
+    def gathered(k, xf, cf):
+        arrived(held.at[k, xf, cf], g_recv.at[k, xf, cf])
+
+    for k in range(1, nz):
+        remote(meta.at[0], meta.at[k], meta_send.at[k], meta_recv.at[k], along(k))
+    loads[0].wait()
+    for k in range(1, nz):
+        remote(held.at[0, 0, 0], held.at[k, 0, 0], gz_send.at[k], g_recv.at[k, 0, 0], along(k))
+    gather_core(0, 0)
+    for k in range(1, nz):
+        arrived(meta.at[k], meta_recv.at[k])
+    remote(meta.at[0:nz], meta.at[nz : 2 * nz], meta_send.at[0], meta_recv.at[0], across)
+    gather_across(0)
+    arrived(meta.at[nz : 2 * nz], meta_recv.at[0])
+    remote(meta.at[0 : 2 * nz], meta.at[2 * nz : 4 * nz], meta_send.at[nz], meta_recv.at[nz], sibling)
+    arrived(meta.at[2 * nz : 4 * nz], meta_recv.at[nz])
+    routed_weights(meta, capacity, weights, place, nz)
+    loads[1].wait()
+    loads[2].wait()
+
+    def work(k, xf):
+        gathered(k, xf, 1)
+        rows = held.at[k, xf]
+        slot = (xf * nz + k, (2 + xf) * nz + k)
+        block_work(rows, hidden, up, down, weights, slot, keep.at[k, xf], give.at[k, xf])
+        remote(give.at[k, xf], from_core.at[k, xf], rc_send.at[k, xf], rc_recv.at[k, xf], sibling)
+
+    def sum_for_across(k):
+        arrived(from_core.at[k, 1], rc_recv.at[k, 1])
+        add_rows(keep.at[k, 1], keep.at[k, 1], from_core.at[k, 1])
+        remote(keep.at[k, 1], from_x.at[k], rx_send.at[k], rx_recv.at[k], across)
+
+    def sum_for_along(k):
+        arrived(from_core.at[k, 0], rc_recv.at[k, 0])
+        arrived(from_x.at[k], rx_recv.at[k])
+        add_rows(keep.at[k, 0], keep.at[k, 0], from_core.at[k, 0], from_x.at[k])
+        remote(keep.at[k, 0], from_z.at[k], rz_send.at[k], rz_recv.at[k], along(nz - k))
+
+    work(0, 0)
+    for k in range(1, nz):
+        gathered(k, 0, 0)
+        gather_across(k)
+        gather_core(k, 0)
+        gathered(k - 1, 1, 0)
+        gather_core(k - 1, 1)
+        work(k - 1, 1)
+        work(k, 0)
+        sum_for_across(k - 1)
+        if k >= 3:
+            sum_for_along(k - 2)
+    gathered(nz - 1, 1, 0)
+    gather_core(nz - 1, 1)
+    work(nz - 1, 1)
+    if nz >= 3:
+        sum_for_along(nz - 2)
+    sum_for_across(nz - 1)
+    if nz >= 2:
+        sum_for_along(nz - 1)
+    arrived(from_core.at[0, 0], rc_recv.at[0, 0])
+    arrived(from_x.at[0], rx_recv.at[0])
+    for k in range(1, nz):
+        arrived(from_z.at[k], rz_recv.at[k])
+    add_rows(out, keep.at[0, 0], from_core.at[0, 0], from_x.at[0], *[from_z.at[k] for k in range(1, nz)])
+    for copy in sent:
+        copy.wait_send()
+
+
+def fused(size, tokens, expert_ids, gate_numer, capacity, up_weight, down_weight):
+    nz = size // 4
+    block, columns = tokens.shape
+    inner = up_weight.shape[2]
+    routing = jnp.concatenate([expert_ids, gate_numer], axis=1).astype(jnp.bfloat16).T
+    anywhere = pl.BlockSpec(memory_space=pl.ANY)
+    near = pl.BlockSpec(memory_space=pltpu.VMEM)
+    wide = jnp.bfloat16
+    dma = pltpu.SemaphoreType.DMA
+    return pl.pallas_call(
+        functools.partial(kernel, nz),
+        out_shape=jax.ShapeDtypeStruct((block, columns), tokens.dtype),
+        in_specs=[anywhere, near, pl.BlockSpec(memory_space=pltpu.SMEM), anywhere, anywhere],
+        out_specs=near,
+        scratch_shapes=[
+            pltpu.VMEM((nz, 2, 2, block, columns), wide),
+            pltpu.VMEM((size,) + routing.shape, wide),
+            pltpu.VMEM((columns, inner), wide),
+            pltpu.VMEM((inner, columns), wide),
+            pltpu.VMEM((2 * block, inner), wide),
+            pltpu.VMEM((block, block), jnp.float32),
+            pltpu.VMEM((nz, 2, block, columns), wide),
+            pltpu.VMEM((nz, 2, block, columns), wide),
+            pltpu.VMEM((nz, 2, block, columns), wide),
+            pltpu.VMEM((nz, block, columns), wide),
+            pltpu.VMEM((nz, block, columns), wide),
+            dma((3,)), dma((nz + 1,)), dma((nz + 1,)),
+            dma((nz,)), dma((nz,)), dma((nz, 2)), dma((nz, 2, 2)),
+            dma((nz, 2)), dma((nz, 2)), dma((nz,)), dma((nz,)), dma((nz,)), dma((nz,)),
+        ],
+        compiler_params=pltpu.CompilerParams(
+            collective_id=0, has_side_effects=True, vmem_limit_bytes=56 * 2**20
+        ),
+        cost_estimate=pl.CostEstimate(
+            flops=4 * size * block * columns * inner, bytes_accessed=4 * columns * inner, transcendentals=0
+        ),
+    )(tokens, routing, capacity, up_weight, down_weight)
+
+
 def solution(mesh):
+    size = mesh.shape["expert"]
+    fits = mesh.shape["tensor"] == 1 and size % 4 == 0 and size <= 16
+    local = functools.partial(fused, size) if fits else general
     in_specs = (
         P(("group", "expert"), "tensor"),
         P(("group", "expert"), None),

time: 476 us -> 145 us (0.30)
  blocking collectives: 198 us -> 0 us
  waiting for transfers between devices: 181 us -> 0 us
  Pallas kernels: 0 us -> 141 us
  local copies, waits for them, and re-layouts: 52.7 us -> 1.88 us
  matrix products: 20.4 us -> 0 us
  other arithmetic: 14.7 us -> 1.97 us
  starting transfers between devices: 6.15 us -> 0 us
    all_to_all x1 -> x0, blocking collectives: 189 us -> none  [local(): lax.all_to_all(outgoing, 'expert', split_axis=0, concat_axis=0, tiled=True)]
    all_to_all x1 -> x0, waiting for transfers between devices: 181 us -> none  [local(): lax.all_to_all(expert_work(arrived, up_matrix, down_matrix), 'expert', sp...]
    pallas_call x0 -> x1, Pallas kernels: none -> 141 us  [fused(): pl.pallas_call(functools.partial(kernel, nz), out_shape=jax.ShapeDtypeStr...]
    gather x2 -> x0, local copies, waits for them, and re-layouts: 43 us -> none  [the longest x1 25.6 us: local(): picked = returned[chosen, local_rank]]
    dot_general x1 -> x0, matrix products: 20.4 us -> none  [expert_work(): jnp.dot(fragment.reshape(-1, columns), weights_block, preferred_element_t...]
    unnamed x1 -> x0, blocking collectives: 8.24 us -> none
    reduce_sum x4 -> x0, other arithmetic: 8.24 us -> none  [the longest x1 7.33 us: local(): jnp.sum(weighted.reshape(token_rows, per_token, picked.shape[1]), axis=1)]
    all_to_all x1 -> x0, starting transfers between devices: 6.15 us -> none  [local(): lax.all_to_all(expert_work(arrived, up_matrix, down_matrix), 'expert', sp...]
  transfers between devices with their start and end apart: 1 -> 0, of which waited for: 1 -> 0; matrix products, arithmetic and copies ran while one was open for 0% -> 0% of each run, Pallas kernels for 0% -> 0%
where the time goes in v2:
time: 145 us
  Pallas kernels  141 us (97%)
  other arithmetic  1.97 us (1%)
  local copies, waits for them, and re-layouts  1.88 us (1%)
    pallas_call x1, Pallas kernels, fused(): pl.pallas_call(functools.partial(kernel, nz), out_shape=jax.ShapeDtypeStr...  141 us

profile of v2, /device:TPU:26, one launch (start us, length us, event | category | flops | bytes accessed | tf_op | source)
XLA Modules:
  0.0 144.6 jit_solution(7039478456874374802)
XLA Ops:
  0.0 0.7 convert.6
  0.7 0.7 convert.7
  1.4 0.6 maximum_bitcast_fusion.meta_in
  2.0 140.7 %shard_map.64 = bf16[128,2048]{1,0:T(8,128)(2,1)} custom-call(bf16[128,2048]{1,0:T(8,128)(2,1)} %tokens_hbm.1, bf16[16,128]{1,0:T(8,128)(2,1)} %maximum_bitcast_fusion.meta_in, s32[16]{0:T(128)} %capacity.1, bf16[1,2048,768]{2,1,0:T(8,128)(2,1)} %up_hbm.1, bf16[1,768,2048]{2,1,0:T(8,128)(2,1)} %down_hbm.1), custom_call_target="tpu_custom_call" | custom-call | flops 12884901888 | bytes 6291456 | tf_op jit(solution)/shard_map/pallas_call | solution.py:273
  142.7 1.9 %copy.8 = bf16[128,2048]{1,0:T(8,128)(2,1)} copy(bf16[128,2048]{1,0:T(8,128)(2,1)} %shard_map.64) | data formatting | bytes 1048576

commit v3 on v2

--- a/solution.py
+++ b/solution.py
@@ -88,6 +88,15 @@
         for part in parts[1:]:
             total = total + part[rows, :].astype(jnp.float32)
         dst[rows, :] = total.astype(dst.dtype)
+
+
+def nearest(at, nz):
+    offsets = [0]
+    for distance in range(1, nz):
+        for source in (at - distance, at + distance):
+            if 0 <= source < nz:
+                offsets.append((at - source) % nz)
+    return offsets
 
 
 def routed_weights(meta, capacity, weights, place, nz):
@@ -133,8 +142,9 @@
         v = jnp.dot(rows[...].reshape(2 * block, rows.shape[-1]), up[:, cols], preferred_element_type=jnp.float32)
         hidden[:, cols] = (v / (1.0 + jnp.exp(-v))).astype(jnp.bfloat16)
 
-    mine = weights[:, slot[0] : slot[0] + 1]
-    other = weights[:, slot[1] : slot[1] + 1]
+    lane = lax.broadcasted_iota(jnp.int32, weights.shape, 1)
+    mine = jnp.sum(jnp.where(lane == slot[0], weights[...], 0.0), axis=1, keepdims=True)
+    other = jnp.sum(jnp.where(lane == slot[1], weights[...], 0.0), axis=1, keepdims=True)
 
     @pl.loop(0, down.shape[1] // width)
     def _(i):
@@ -159,13 +169,16 @@
     def along(k):
         return lax.rem(place + 4 * k, 4 * nz)
 
-    def remote(src, dst, send, recv, target):
+    def remote(src, dst, send, recv, target, when=None):
         copy = pltpu.make_async_remote_copy(
             src_ref=src, dst_ref=dst, send_sem=send, recv_sem=recv,
             device_id={"expert": target}, device_id_type=pl.DeviceIdType.MESH,
         )
-        copy.start()
-        sent.append(copy)
+        if when is None:
+            copy.start()
+        else:
+            pl.when(when)(copy.start)
+        sent.append((copy, when))
 
     def arrived(ref, sem):
         pltpu.make_async_copy(ref, ref, sem).wait()
@@ -188,20 +201,49 @@
         )
     pl.semaphore_wait(barrier, len(partners))
 
-    def gather_across(k):
-        remote(held.at[k, 0, 0], held.at[k, 1, 0], gx_send.at[k], g_recv.at[k, 1, 0], across)
-
-    def gather_core(k, xf):
-        remote(held.at[k, xf, 0], held.at[k, xf, 1], gc_send.at[k, xf], g_recv.at[k, xf, 1], sibling)
-
-    def gathered(k, xf, cf):
+    steps = [
+        functools.reduce(lambda a, s: a + s, [jnp.where(z == at, nearest(at, nz)[i], 0) for at in range(nz)])
+        for i in range(nz)
+    ]
+
+    def gather_along(i):
+        k = steps[i]
+        rising = k <= z
+        step = jnp.where(rising, 1, -1)
+        target = jnp.clip(z + step, 0, nz - 1)
+        slot = jnp.clip(k + step, 0, nz - 1)
+        remote(
+            held.at[k, 0, 0], held.at[slot, 0, 0], gz_send.at[i], g_recv.at[slot, 0, 0],
+            place + 4 * (target - z), target != z,
+        )
+
+    def gather_own():
+        up_z, down_z = jnp.minimum(z + 1, nz - 1), jnp.maximum(z - 1, 0)
+        remote(
+            held.at[0, 0, 0], held.at[1 % nz, 0, 0], gz_send.at[0], g_recv.at[1 % nz, 0, 0],
+            place + 4 * (up_z - z), up_z != z,
+        )
+        remote(
+            held.at[0, 0, 0], held.at[nz - 1, 0, 0], gz_send.at[nz], g_recv.at[nz - 1, 0, 0],
+            place + 4 * (down_z - z), down_z != z,
+        )
+
+    def gather_across(i):
+        k = steps[i]
+        remote(held.at[k, 0, 0], held.at[k, 1, 0], gx_send.at[i], g_recv.at[k, 1, 0], across)
+
+    def gather_core(i, xf):
+        k = steps[i]
+        remote(held.at[k, xf, 0], held.at[k, xf, 1], gc_send.at[i, xf], g_recv.at[k, xf, 1], sibling)
+
+    def gathered(i, xf, cf):
+        k = steps[i]
         arrived(held.at[k, xf, cf], g_recv.at[k, xf, cf])
 
     for k in range(1, nz):
         remote(meta.at[0], meta.at[k], meta_send.at[k], meta_recv.at[k], along(k))
     loads[0].wait()
-    for k in range(1, nz):
-        remote(held.at[0, 0, 0], held.at[k, 0, 0], gz_send.at[k], g_recv.at[k, 0, 0], along(k))
+    gather_own()
     gather_core(0, 0)
     for k in range(1, nz):
         arrived(meta.at[k], meta_recv.at[k])
@@ -214,51 +256,58 @@
     loads[1].wait()
     loads[2].wait()
 
-    def work(k, xf):
-        gathered(k, xf, 1)
-        rows = held.at[k, xf]
+    def work(i, xf):
+        gathered(i, xf, 1)
+        k = steps[i]
         slot = (xf * nz + k, (2 + xf) * nz + k)
-        block_work(rows, hidden, up, down, weights, slot, keep.at[k, xf], give.at[k, xf])
-        remote(give.at[k, xf], from_core.at[k, xf], rc_send.at[k, xf], rc_recv.at[k, xf], sibling)
-
-    def sum_for_across(k):
-        arrived(from_core.at[k, 1], rc_recv.at[k, 1])
-        add_rows(keep.at[k, 1], keep.at[k, 1], from_core.at[k, 1])
-        remote(keep.at[k, 1], from_x.at[k], rx_send.at[k], rx_recv.at[k], across)
-
-    def sum_for_along(k):
-        arrived(from_core.at[k, 0], rc_recv.at[k, 0])
-        arrived(from_x.at[k], rx_recv.at[k])
-        add_rows(keep.at[k, 0], keep.at[k, 0], from_core.at[k, 0], from_x.at[k])
-        remote(keep.at[k, 0], from_z.at[k], rz_send.at[k], rz_recv.at[k], along(nz - k))
+        block_work(held.at[k, xf], hidden, up, down, weights, slot, keep.at[i, xf], give.at[i, xf])
+        remote(give.at[i, xf], from_core.at[i, xf], rc_send.at[i, xf], rc_recv.at[i, xf], sibling)
+
+    def sum_for_across(i):
+        arrived(from_core.at[i, 1], rc_recv.at[i, 1])
+        add_rows(keep.at[i, 1], keep.at[i, 1], from_core.at[i, 1])
+        remote(keep.at[i, 1], from_x.at[i], rx_send.at[i], rx_recv.at[i], across)
+
+    def sum_for_along(i):
+        arrived(from_core.at[i, 0], rc_recv.at[i, 0])
+        arrived(from_x.at[i], rx_recv.at[i])
+        add_rows(keep.at[i, 0], keep.at[i, 0], from_core.at[i, 0], from_x.at[i])
+        k = steps[i]
+        remote(keep.at[i, 0], from_z.at[k], rz_send.at[i], rz_recv.at[k], along(nz - k))
 
     work(0, 0)
-    for k in range(1, nz):
-        gathered(k, 0, 0)
-        gather_across(k)
-        gather_core(k, 0)
-        gathered(k - 1, 1, 0)
-        gather_core(k - 1, 1)
-        work(k - 1, 1)
-        work(k, 0)
-        sum_for_across(k - 1)
-        if k >= 3:
-            sum_for_along(k - 2)
+    for i in range(1, nz):
+        gathered(i, 0, 0)
+        gather_along(i)
+        gather_across(i)
+        gather_core(i, 0)
+        gathered(i - 1, 1, 0)
+        gather_core(i - 1, 1)
+        work(i - 1, 1)
+        work(i, 0)
+        if i >= 2:
+            sum_for_across(i - 1)
+        if i >= 3:
+            sum_for_along(i - 2)
     gathered(nz - 1, 1, 0)
     gather_core(nz - 1, 1)
     work(nz - 1, 1)
     if nz >= 3:
         sum_for_along(nz - 2)
-    sum_for_across(nz - 1)
     if nz >= 2:
+        sum_for_across(nz - 1)
+        sum_for_across(0)
         sum_for_along(nz - 1)
     arrived(from_core.at[0, 0], rc_recv.at[0, 0])
     arrived(from_x.at[0], rx_recv.at[0])
     for k in range(1, nz):
         arrived(from_z.at[k], rz_recv.at[k])
     add_rows(out, keep.at[0, 0], from_core.at[0, 0], from_x.at[0], *[from_z.at[k] for k in range(1, nz)])
-    for copy in sent:
-        copy.wait_send()
+    for copy, when in sent:
+        if when is None:
+            copy.wait_send()
+        else:
+            pl.when(when)(copy.wait_send)
 
 
 def fused(size, tokens, expert_ids, gate_numer, capacity, up_weight, down_weight):
@@ -288,7 +337,7 @@
             pltpu.VMEM((nz, block, columns), wide),
             pltpu.VMEM((nz, block, columns), wide),
             dma((3,)), dma((nz + 1,)), dma((nz + 1,)),
-            dma((nz,)), dma((nz,)), dma((nz, 2)), dma((nz, 2, 2)),
+            dma((nz + 1,)), dma((nz,)), dma((nz, 2)), dma((nz, 2, 2)),
             dma((nz, 2)), dma((nz, 2)), dma((nz,)), dma((nz,)), dma((nz,)), dma((nz,)),
         ],
         compiler_params=pltpu.CompilerParams(

time: 145 us -> 128 us (0.88)
  Pallas kernels: 141 us -> 124 us
    pallas_call x1, Pallas kernels: 141 us -> 124 us  [fused(): pl.pallas_call(functools.partial(kernel, nz), out_shape=jax.ShapeDtypeStr...]
where the time goes in v3:
time: 128 us; the launch traced here: 127 us
  Pallas kernels  124 us (97%)
  other arithmetic  1.97 us (2%)
  local copies, waits for them, and re-layouts  1.88 us (1%)
    pallas_call x1, Pallas kernels, fused(): pl.pallas_call(functools.partial(kernel, nz), out_shape=jax.ShapeDtypeStr...  124 us

profile of v3, /device:TPU:26, one launch (start us, length us, event | category | flops | bytes accessed | tf_op | source)
XLA Modules:
  0.0 127.5 jit_solution(7768219821252901526)
XLA Ops:
  0.0 0.7 convert.6
  0.7 0.7 convert.7
  1.4 0.6 maximum_bitcast_fusion.meta_in
  2.0 123.6 %shard_map.64 = bf16[128,2048]{1,0:T(8,128)(2,1)} custom-call(bf16[128,2048]{1,0:T(8,128)(2,1)} %tokens_hbm.1, bf16[16,128]{1,0:T(8,128)(2,1)} %maximum_bitcast_fusion.meta_in, s32[16]{0:T(128)} %capacity.1, bf16[1,2048,768]{2,1,0:T(8,128)(2,1)} %up_hbm.1, bf16[1,768,2048]{2,1,0:T(8,128)(2,1)} %down_hbm.1), custom_call_target="tpu_custom_call" | custom-call | flops 12884901888 | bytes 6291456 | tf_op jit(solution)/shard_map/pallas_call | solution.py:322
  125.6 1.9 %copy.8 = bf16[128,2048]{1,0:T(8,128)(2,1)} copy(bf16[128,2048]{1,0:T(8,128)(2,1)} %shard_map.64) | data formatting | bytes 1048576

commit v4 on v3

--- a/solution.py
+++ b/solution.py
@@ -184,6 +184,7 @@
         pltpu.make_async_copy(ref, ref, sem).wait()
 
     sent = []
+    parts = 2
     loads = [
         pltpu.make_async_copy(tokens_hbm, held.at[0, 0, 0], local_sem.at[0]),
         pltpu.make_async_copy(up_hbm.at[0], up, local_sem.at[1]),
@@ -263,17 +264,23 @@
         block_work(held.at[k, xf], hidden, up, down, weights, slot, keep.at[i, xf], give.at[i, xf])
         remote(give.at[i, xf], from_core.at[i, xf], rc_send.at[i, xf], rc_recv.at[i, xf], sibling)
 
+    pieces = [pl.ds(at * (block // parts), block // parts) for at in range(parts)]
+
     def sum_for_across(i):
         arrived(from_core.at[i, 1], rc_recv.at[i, 1])
-        add_rows(keep.at[i, 1], keep.at[i, 1], from_core.at[i, 1])
-        remote(keep.at[i, 1], from_x.at[i], rx_send.at[i], rx_recv.at[i], across)
+        for p, rows in enumerate(pieces):
+            mine = keep.at[i, 1, rows]
+            add_rows(mine, mine, from_core.at[i, 1, rows])
+            remote(mine, from_x.at[i, rows], rx_send.at[i, p], rx_recv.at[i, p], across)
 
     def sum_for_along(i):
         arrived(from_core.at[i, 0], rc_recv.at[i, 0])
-        arrived(from_x.at[i], rx_recv.at[i])
-        add_rows(keep.at[i, 0], keep.at[i, 0], from_core.at[i, 0], from_x.at[i])
-        k = steps[i]
-        remote(keep.at[i, 0], from_z.at[k], rz_send.at[i], rz_recv.at[k], along(nz - k))
+        k = steps[i]
+        for p, rows in enumerate(pieces):
+            mine = keep.at[i, 0, rows]
+            arrived(from_x.at[i, rows], rx_recv.at[i, p])
+            add_rows(mine, mine, from_core.at[i, 0, rows], from_x.at[i, rows])
+            remote(mine, from_z.at[k, rows], rz_send.at[i, p], rz_recv.at[k, p], along(nz - k))
 
     work(0, 0)
     for i in range(1, nz):
@@ -299,10 +306,12 @@
         sum_for_across(0)
         sum_for_along(nz - 1)
     arrived(from_core.at[0, 0], rc_recv.at[0, 0])
-    arrived(from_x.at[0], rx_recv.at[0])
-    for k in range(1, nz):
-        arrived(from_z.at[k], rz_recv.at[k])
-    add_rows(out, keep.at[0, 0], from_core.at[0, 0], from_x.at[0], *[from_z.at[k] for k in range(1, nz)])
+    for p, rows in enumerate(pieces):
+        arrived(from_x.at[0, rows], rx_recv.at[0, p])
+        for k in range(1, nz):
+            arrived(from_z.at[k, rows], rz_recv.at[k, p])
+        others = [from_z.at[k, rows] for k in range(1, nz)]
+        add_rows(out.at[rows], keep.at[0, 0, rows], from_core.at[0, 0, rows], from_x.at[0, rows], *others)
     for copy, when in sent:
         if when is None:
             copy.wait_send()
@@ -338,7 +347,7 @@
             pltpu.VMEM((nz, block, columns), wide),
             dma((3,)), dma((nz + 1,)), dma((nz + 1,)),
             dma((nz + 1,)), dma((nz,)), dma((nz, 2)), dma((nz, 2, 2)),
-            dma((nz, 2)), dma((nz, 2)), dma((nz,)), dma((nz,)), dma((nz,)), dma((nz,)),
+            dma((nz, 2)), dma((nz, 2)), dma((nz, 2)), dma((nz, 2)), dma((nz, 2)), dma((nz, 2)),
         ],
         compiler_params=pltpu.CompilerParams(
             collective_id=0, has_side_effects=True, vmem_limit_bytes=56 * 2**20

time: 128 us -> 123 us (0.961)
  Pallas kernels: 124 us -> 119 us
    pallas_call x1, Pallas kernels: 124 us -> 119 us  [fused(): pl.pallas_call(functools.partial(kernel, nz), out_shape=jax.ShapeDtypeStr...]
where the time goes in v4:
time: 123 us
  Pallas kernels  119 us (97%)
  other arithmetic  1.97 us (2%)
  local copies, waits for them, and re-layouts  1.88 us (2%)
    pallas_call x1, Pallas kernels, fused(): pl.pallas_call(functools.partial(kernel, nz), out_shape=jax.ShapeDtypeStr...  119 us

profile of v4, /device:TPU:26, one launch (start us, length us, event | category | flops | bytes accessed | tf_op | source)
XLA Modules:
  0.0 123.0 jit_solution(6396763341047475679)
XLA Ops:
  0.0 0.7 convert.6
  0.7 0.7 convert.7
  1.4 0.6 maximum_bitcast_fusion.meta_in
  2.0 119.1 %shard_map.64 = bf16[128,2048]{1,0:T(8,128)(2,1)} custom-call(bf16[128,2048]{1,0:T(8,128)(2,1)} %tokens_hbm.1, bf16[16,128]{1,0:T(8,128)(2,1)} %maximum_bitcast_fusion.meta_in, s32[16]{0:T(128)} %capacity.1, bf16[1,2048,768]{2,1,0:T(8,128)(2,1)} %up_hbm.1, bf16[1,768,2048]{2,1,0:T(8,128)(2,1)} %down_hbm.1), custom_call_target="tpu_custom_call" | custom-call | flops 12884901888 | bytes 6291456 | tf_op jit(solution)/shard_map/pallas_call | solution.py:331
  121.1 1.9 %copy.8 = bf16[128,2048]{1,0:T(8,128)(2,1)} copy(bf16[128,2048]{1,0:T(8,128)(2,1)} %shard_map.64) | data formatting | bytes 1048576

commit v5 on v4

--- a/solution.py
+++ b/solution.py
@@ -184,7 +184,7 @@
         pltpu.make_async_copy(ref, ref, sem).wait()
 
     sent = []
-    parts = 2
+    parts = 4
     loads = [
         pltpu.make_async_copy(tokens_hbm, held.at[0, 0, 0], local_sem.at[0]),
         pltpu.make_async_copy(up_hbm.at[0], up, local_sem.at[1]),
@@ -347,7 +347,7 @@
             pltpu.VMEM((nz, block, columns), wide),
             dma((3,)), dma((nz + 1,)), dma((nz + 1,)),
             dma((nz + 1,)), dma((nz,)), dma((nz, 2)), dma((nz, 2, 2)),
-            dma((nz, 2)), dma((nz, 2)), dma((nz, 2)), dma((nz, 2)), dma((nz, 2)), dma((nz, 2)),
+            dma((nz, 2)), dma((nz, 2)), dma((nz, 4)), dma((nz, 4)), dma((nz, 4)), dma((nz, 4)),
         ],
         compiler_params=pltpu.CompilerParams(
             collective_id=0, has_side_effects=True, vmem_limit_bytes=56 * 2**20

time: 123 us -> 122 us (level)
  no operation moved by 1% of the time
where the time goes in v5:
time: 122 us
  Pallas kernels  118 us (97%)
  other arithmetic  1.97 us (2%)
  local copies, waits for them, and re-layouts  1.88 us (2%)
    pallas_call x1, Pallas kernels, fused(): pl.pallas_call(functools.partial(kernel, nz), out_shape=jax.ShapeDtypeStr...  118 us

profile of v5, /device:TPU:26, one launch (start us, length us, event | category | flops | bytes accessed | tf_op | source)
XLA Modules:
  0.0 121.9 jit_solution(17390084971189916512)
XLA Ops:
  0.0 0.7 convert.6
  0.7 0.7 convert.7
  1.4 0.6 maximum_bitcast_fusion.meta_in
  2.0 118.1 %shard_map.64 = bf16[128,2048]{1,0:T(8,128)(2,1)} custom-call(bf16[128,2048]{1,0:T(8,128)(2,1)} %tokens_hbm.1, bf16[16,128]{1,0:T(8,128)(2,1)} %maximum_bitcast_fusion.meta_in, s32[16]{0:T(128)} %capacity.1, bf16[1,2048,768]{2,1,0:T(8,128)(2,1)} %up_hbm.1, bf16[1,768,2048]{2,1,0:T(8,128)(2,1)} %down_hbm.1), custom_call_target="tpu_custom_call" | custom-call | flops 12884901888 | bytes 6291456 | tf_op jit(solution)/shard_map/pallas_call | solution.py:331
  120.0 1.9 %copy.8 = bf16[128,2048]{1,0:T(8,128)(2,1)} copy(bf16[128,2048]{1,0:T(8,128)(2,1)} %shard_map.64) | data formatting | bytes 1048576
